TPU v7x, 32 devices: a whole 2x2x4 slice. The times are simulated.
32 devices in a mesh: groups: 2 (over x), region: 16 (over z, y, core).
Axes of the slice: x: 2, y: 2, z: 4, core: 2. Of those that a mesh axis runs over, the one named last changes fastest.
Arguments:
- obs_pos: float32 [512, 2, 256], P(('groups', 'region')), parts along dimension 0, may hold values from 0 to 230400, as said below
- obs_sigma: float32 [512, 256], P(('groups', 'region')), parts along dimension 0, may hold values from 0.5 to 1.2
- obs_error: float32 [512, 256], P(('groups', 'region')), parts along dimension 0, may hold values from 0.2 to 2
- innovation: float32 [512, 64, 256], P(('groups', 'region')), parts along dimension 0, may hold values from -6 to 6
- obs_count: int32 [512], P(('groups', 'region')), parts along dimension 0, may hold values from 1 to 256
- pair_list: int32 [2, 3072], P(None, ('groups', 'region')), parts along dimension 1, may hold values from 0 to 255, as said below
- pair_live: int32 [32], P(('groups', 'region')), parts along dimension 0, may hold values from 16 to 96
Outputs:
- solution: float32 [512, 64, 256], P(('groups', 'region')), parts along dimension 0
- residual: float32 [512, 64, 256], P(('groups', 'region')), parts along dimension 0
There are 2 independent parts, one for each index of `groups`. A program takes and returns all parts, laid end to end along the dimension named above; each array names one. Nothing has to cross between parts.
Inputs may be any that keep to these rules, and one draw needn't show every extreme that they name: `obs_pos`: block b's observations lie in cell b, an interval of the first coordinate 300 to 900 km long; cells follow one another without gaps in block order from 0; the second coordinate lies in 0 to 600 km. `pair_list`: device k's 96 slots hold pairs (i, j) with i among its 16 blocks and i <= j <= i + 5; its first pair_live[k] slots list, each once, every pair of such an i with a block j >= i whose cells lie less than 1500 km apart (i = j included); the other slots hold (k * 16, k * 16).
All inputs are finite; a program needn't handle non-finite values.
Results may differ from a plain program's by a relative error of at most 0.0003.
Values sent between devices are 32-bit elements; how exact they have to be, the bound alone decides.
No kernel may reach another device: no remote copies, remote signals or barrier semaphores. Data moves between devices by JAX's collectives and lax.ppermute only.
A program may use at most 64 MiB of HBM per device.

v0:
```python
import functools

import jax
import jax.numpy as jnp
from jax import lax
from jax.experimental import pallas as pl
from jax.experimental.pallas import tpu as pltpu
from jax.sharding import PartitionSpec as P

REACH = 5
CUTOFF_KM = 1500.0
SCALE_KM = 1000.0
LOG2E = 1.4426950408889634
UNIT = LOG2E / SCALE_KM
TAPER = 1.0 / (CUTOFF_KM * UNIT)
LIMIT = CUTOFF_KM * UNIT
CH = 256
LN = 128
GROUP = 4
BATCH = 8
SPAN = 7
TINY = 1e-30
F32, BF16, I32 = jnp.float32, jnp.bfloat16, jnp.int32
VM = pl.BlockSpec(memory_space=pltpu.VMEM)
SM = pl.BlockSpec(memory_space=pltpu.SMEM)
HB = pl.BlockSpec(memory_space=pltpu.HBM)
MB = 1 << 20
OWN_HELD = 56
SIDE_HELD = 24


def lanes(shape):
    return lax.broadcasted_iota(I32, shape, len(shape) - 1)


def at(start, size=CH):
    return pl.ds(pl.multiple_of(start, LN), size)


def pack_block(rows, count, offset, dst):
    base = (offset // LN) * LN
    shift = offset - base
    lane = lanes((rows.shape[0], LN))
    low = pltpu.roll(jnp.where(lane < count, rows[:, :LN], 0.0), shift, 1)
    high = pltpu.roll(jnp.where(lane + LN < count, rows[:, LN:], 0.0), shift, 1)
    before = lane < shift
    dst[:, at(base, LN)] = jnp.where(before, dst[:, at(base, LN)], low)
    dst[:, at(base + LN, LN)] = jnp.where(before, low, high)
    dst[:, at(base + 2 * LN, LN)] = jnp.where(before, high, 0.0)
    dst[:, at(base + 3 * LN, LN)] = jnp.zeros_like(low)


def split(values):
    high = values.astype(BF16)
    return high, (values - high.astype(F32)).astype(BF16)


def put_split(values, dst, place):
    high, low = split(values)
    half = values.shape[0]
    dst[place, :half, :] = high
    dst[place, half:, :] = low


def columns(row):
    parts = [jnp.broadcast_to(row[:, k : k + LN], (LN, LN)).T for k in (0, LN)]
    return jnp.concatenate(parts, axis=0)


def build(col_x, col_y, place, row_x, row_y, tile_ref, slot):
    strip = 32
    for top in range(0, CH, strip):
        for left in range(0, CH, LN):
            dx = col_x[place, top : top + strip, :] - row_x[:, left : left + LN]
            dy = col_y[place, top : top + strip, :] - row_y[:, left : left + LN]
            square = jnp.maximum(dx * dx + dy * dy, TINY)
            distance = square * lax.rsqrt(square)
            tapered = jnp.maximum(1.0 - distance * TAPER, 0.0)
            value = jnp.exp2(-distance) * (tapered * tapered)
            high, low = split(value)
            tile_ref[slot, top : top + strip, left : left + LN] = high
            tile_ref[slot, CH + top : CH + top + strip, left : left + LN] = low


def product(parts_ref, place, tile_ref, slot, transposed):
    dims = (((1,), (1 if transposed else 0,)), ((), ()))
    both = parts_ref[place]
    half = both.shape[0] // 2
    wide = lax.dot_general(both, tile_ref[slot, :CH, :], dims, preferred_element_type=F32)
    fine = lax.dot_general(both[:half], tile_ref[slot, CH:, :], dims, preferred_element_type=F32)
    return wide[:half] + wide[half:] + fine


def own_product(t, total, down, across, parts_ref, tile_ref, slot, acc):
    i, j = down[t], across[t]
    here = (t < total).astype(F32)
    forward = product(parts_ref, i, tile_ref, slot, False)
    backward = product(parts_ref, j, tile_ref, slot, True)
    acc[:, at(j * CH)] += here * forward
    acc[:, at(i * CH)] += here * backward


def diagonal_product(t, total, parts_ref, tile_ref, slot, acc):
    here = (t < total).astype(F32)
    i = jnp.minimum(t, total - 1)
    acc[:, at(i * CH)] += here * product(parts_ref, i, tile_ref, slot, False)


def edge_product(t, total, down, across, parts_ref, tile_ref, slot, acc):
    here = (t < total).astype(F32)
    acc[:, at(across[t] * CH)] += here * product(parts_ref, down[t], tile_ref, slot, False)


def sweep(total, held, make, multiply):
    pairs = (total + 1) // 2
    full = jnp.minimum(total, 2 * held) // BATCH

    def many(p, carry):
        for half in (make, multiply):
            for u in range(BATCH):
                if half is not None:
                    half(BATCH * p + u, u % 2, BATCH // 2 * p + u // 2)
        return carry

    def few(p, carry):
        for half in (make, multiply):
            for u in range(2):
                if half is not None:
                    half(2 * p + u, u, jnp.minimum(p, held))
        return carry

    lax.fori_loop(0, full, many, 0)
    end = pairs if make is not None else jnp.minimum(pairs, held)
    lax.fori_loop(full * (BATCH // 2), end, few, 0)


def sweep_rest(total, held, make, multiply):
    def few(p, carry):
        for half in (make, multiply):
            for u in range(2):
                half(2 * p + u, u, 0)
        return carry

    lax.fori_loop(held, (total + 1) // 2, few, 0)


def remake(t, down, across, down_geo, geo, col_x, col_y, ref):
    where = at(down[t] * CH)
    col_x[0] = columns(down_geo[0:1, where])
    col_y[0] = columns(down_geo[1:2, where])
    where = at(across[t] * CH)
    build(col_x, col_y, 0, geo[0:1, where], geo[1:2, where], ref, 0)


def prepare_kernel(innov_in, pos_in, sigma_in, err_in, count_in, first_out, second_out, vec, geo,
                   parts, col_x, col_y, ints, floats, down, across, innov, pos, sigma, err, count,
                   sems):
    blocks, members = innov.shape[0], innov.shape[1]
    odd = lax.rem(lax.axis_index("region"), 2)
    starts = ((1 - odd) * (blocks - REACH), odd * (blocks - REACH))
    ends = tuple(zip(starts, (first_out, second_out)))
    small = [(pos_in, pos), (sigma_in, sigma), (err_in, err), (count_in, count)]
    large = [(innov_in, innov)]
    for start, dst in ends:
        large.append((innov_in.at[pl.ds(start, REACH)], dst.at[:, pl.ds(0, members), :]))
    copies = [
        pltpu.make_async_copy(src, dst, sems.at[k]) for k, (src, dst) in enumerate(small + large)
    ]
    for copy in copies:
        copy.start()
    for copy in copies[: len(small)]:
        copy.wait()
    for start, dst in ends:
        for b in range(REACH):
            number = jnp.full((1, CH), count[start + b].astype(F32))
            rest = jnp.zeros((4, CH), F32)
            dst[b, members:, :] = jnp.concatenate(
                [pos[start + b], sigma[pl.ds(start + b, 1), :], number, rest], axis=0
            )
    origin = pos[0, 0:1, 0:1]
    floats[0] = jnp.max(origin)

    def pack_geo(b, offset):
        ints[b] = offset
        pair = pos[b]
        rows = jnp.concatenate(
            [
                (pair[0:1] - origin) * UNIT,
                pair[1:2] * UNIT,
                sigma[pl.ds(b, 1), :],
                err[pl.ds(b, 1), :],
                jnp.zeros((4, CH), F32),
            ],
            axis=0,
        )
        pack_block(rows, count[b], offset, geo)
        return offset + count[b]

    size = lax.fori_loop(0, blocks, pack_geo, jnp.int32(0), unroll=4)
    ints[blocks] = size
    chunks = (size + CH - 1) // CH
    for copy in copies[len(small) :]:
        copy.wait()

    def pack_vec(b, carry):
        pack_block(innov[b], count[b], ints[b], vec)
        return carry

    lax.fori_loop(0, blocks, pack_vec, 0, unroll=4)

    def prepare(p, carry):
        for u in range(GROUP):
            i = p * GROUP + u
            where = at(i * CH)
            x = geo[0:1, where]
            col_x[i] = columns(x)
            col_y[i] = columns(geo[1:2, where])
            put_split(vec[:, where] * geo[2:3, where], parts, i)
            live = lanes((1, CH)) + i * CH < size
            floats[1 + i] = jnp.min(jnp.where(live, x, 3e38))
            floats[1 + blocks + i] = jnp.max(jnp.where(live, x, -3e38))
        return carry

    lax.fori_loop(0, (chunks + GROUP - 1) // GROUP, prepare, 0)

    def enlist(i, t):
        end = floats[1 + blocks + i]
        for d in range(1, SPAN):
            j = i + d
            start = floats[1 + jnp.minimum(j, blocks - 1)]
            down[t] = i
            across[t] = j
            t = t + jnp.where((j < chunks) & (start - end < LIMIT), 1, 0)
        return t

    total = lax.fori_loop(0, chunks, enlist, jnp.int32(0))
    down[total] = 0
    across[total] = 0
    ints[blocks + 1] = total


def own_kernel(geo, parts, col_x, col_y, ints, down, across, diagonal_ev, diagonal_od, ev, od, acc):
    blocks = parts.shape[0]
    chunks = (ints[blocks] + CH - 1) // CH
    total = ints[blocks + 1]
    acc[...] = jnp.zeros_like(acc)

    def build_at(i, j, ref, slot):
        where = at(j * CH)
        build(col_x, col_y, i, geo[0:1, where], geo[1:2, where], ref, slot)

    def make_diagonal(t, which, slot):
        i = jnp.minimum(t, chunks - 1)
        build_at(i, i, (diagonal_ev, diagonal_od)[which], slot)

    def multiply_diagonal(t, which, slot):
        diagonal_product(t, chunks, parts, (diagonal_ev, diagonal_od)[which], slot, acc)

    sweep(chunks, blocks // 2, make_diagonal, multiply_diagonal)

    def make(t, which, slot):
        build_at(down[t], across[t], (ev, od)[which], slot)

    def multiply(t, which, slot):
        own_product(t, total, down, across, parts, (ev, od)[which], slot, acc)

    sweep(total, ev.shape[0] - 1, make, multiply)


def edge_kernel(from_first, from_second, vec, geo, acc, ints, floats, ev, od, side_geo, side_ints,
                down, across, out, parts, first_out, second_out, side_vec, side_parts, col_x, col_y,
                floats_side):
    members = vec.shape[0]
    blocks = (vec.shape[1] - 2 * CH) // CH
    wide = side_vec.shape[1] // 2
    size = ints[blocks]
    chunks = (size + CH - 1) // CH
    origin = floats[0]
    out[...] = jnp.zeros_like(out)
    side_ends = []
    odd = lax.rem(lax.axis_index("region"), 2)
    for side, ref in enumerate((from_first, from_second)):
        offset = jnp.int32(side * wide)
        for b in range(REACH):
            misc = ref[b, members:, :]
            number = misc[3, 0].astype(I32)
            pack_block(ref[b, :members, :], number, offset, side_vec)
            rows = jnp.concatenate(
                [(misc[0:1] - origin) * UNIT, misc[1:2] * UNIT, misc[2:]], axis=0
            )
            pack_block(rows, number, offset, side_geo)
            offset = offset + number
        side_ends.append(offset)
    down[0] = 0
    across[0] = 0
    side_chunks = [(end - k * wide + CH - 1) // CH for k, end in enumerate(side_ends)]

    def prepare(p, t):
        for h, side in ((2 * p, 0), (2 * p, 1), (2 * p + 1, 0), (2 * p + 1, 1)):
            place = side * (wide // CH) + h
            where = at(place * CH)
            x = side_geo[0:1, where]
            col_x[place] = columns(x)
            col_y[place] = columns(side_geo[1:2, where])
            put_split(side_vec[:, where] * side_geo[2:3, where], side_parts, place)
            live = lanes((1, CH)) + place * CH < side_ends[side]
            floats_side[2 * place] = jnp.min(jnp.where(live, x, 3e38))
            floats_side[2 * place + 1] = jnp.max(jnp.where(live, x, -3e38))
        return t

    lax.fori_loop(0, (jnp.maximum(*side_chunks) + 1) // 2, prepare, 0)
    total = jnp.int32(0)
    for side in range(2):
        ahead = odd == side

        def enlist(h, t, side=side, ahead=ahead):
            place = side * (wide // CH) + h
            low, high = floats_side[2 * place], floats_side[2 * place + 1]
            for d in range(SPAN):
                i = jnp.where(ahead, jnp.maximum(chunks - 1 - d, 0), jnp.minimum(d, chunks - 1))
                apart = jnp.where(ahead, low - floats[1 + blocks + i], floats[1 + i] - high)
                down[t] = place
                across[t] = i
                t = t + jnp.where((apart < LIMIT) & (d < chunks), 1, 0)
            return t

        total = lax.fori_loop(0, side_chunks[side], enlist, total)
    last = jnp.maximum(total - 1, 0)
    down[total] = down[last]
    across[total] = across[last]
    side_ints[0] = total
    for side in range(2):
        side_ints[1 + side] = side_chunks[side]

    def make(t, which, slot):
        where = at(across[t] * CH)
        build(col_x, col_y, down[t], geo[0:1, where], geo[1:2, where], (ev, od)[which], slot)

    def multiply(t, which, slot):
        edge_product(t, total, down, across, side_parts, (ev, od)[which], slot, out)

    sweep(total, ev.shape[0] - 1, make, multiply)

    def finish(i, carry):
        where = at(i * CH)
        scale = geo[2:3, where]
        image = scale * (out[:, where] + acc[:, where]) + geo[3:4, where] * vec[:, where]
        out[:, where] = image
        put_split(image * scale, parts, i)
        return carry

    lax.fori_loop(0, chunks, finish, 0)
    tail = ints[blocks - REACH]
    for start, dst in (((1 - odd) * tail, first_out), (odd * tail, second_out)):
        base = (start // LN) * LN
        shift = start - base
        back = lax.rem(LN - shift, LN)
        keep = lanes((members, LN)) < LN - shift
        turned = pltpu.roll(out[:, at(base, LN)], back, 1)
        for k in range(REACH * CH // LN):
            following = pltpu.roll(out[:, at(base + (k + 1) * LN, LN)], back, 1)
            dst[:, k * LN : (k + 1) * LN] = jnp.where(keep, turned, following)
            turned = following


def halves(values):
    return values[:, :LN] + values[:, LN:]


def lane_sum(values):
    return jnp.sum(values, axis=1, keepdims=True)


def again_kernel(diagonal_ev, diagonal_od, ev, od, parts, geo, vec, image, ints, down, across, acc,
                 known, col_x, col_y, ev_more, od_more):
    blocks = acc.shape[1] // CH - 2
    total = ints[blocks + 1]
    held = ev.shape[0] - 1
    acc[...] = jnp.zeros_like(acc)
    more = (ev_more, od_more)
    chunks = (ints[blocks] + CH - 1) // CH

    def multiply_diagonal(t, which, slot):
        diagonal_product(t, chunks, parts, (diagonal_ev, diagonal_od)[which], slot, acc)

    sweep(chunks, blocks // 2, None, multiply_diagonal)

    def multiply(t, which, slot):
        own_product(t, total, down, across, parts, (ev, od)[which], slot, acc)

    sweep(total, held, None, multiply)

    def make_more(t, which, slot):
        remake(t, down, across, geo, geo, col_x, col_y, more[which])

    def multiply_more(t, which, slot):
        own_product(t, total, down, across, parts, more[which], slot, acc)

    sweep_rest(total, held, make_more, multiply_more)
    members = vec.shape[0]
    zero = jnp.zeros((members, LN), F32)

    def first(i, carry):
        m0, m1 = carry
        r, y = vec[:, at(i * CH)], image[:, at(i * CH)]
        return m0 + halves(r * r), m1 + halves(r * y)

    m0, m1 = (lane_sum(x) for x in lax.fori_loop(0, chunks, first, (zero, zero)))
    mean = jnp.where(m0 > 0, m1 / jnp.where(m0 > 0, m0, 1.0), 0.0)

    def second(i, carry):
        vv, cross, slip = carry
        r, y = vec[:, at(i * CH)], image[:, at(i * CH)]
        z = y - mean * r
        return vv + halves(z * z), cross + halves(z * y), slip + halves(z * r)

    vv, cross, slip = (lane_sum(x) for x in lax.fori_loop(0, chunks, second, (zero, zero, zero)))
    table = jnp.zeros((members, LN), F32)
    lane = lanes((members, LN))
    for k, value in ((0, m0), (1, m1), (2, mean), (3, vv), (5, cross), (6, slip)):
        table = jnp.where(lane == k, value, table)
    known[...] = table


def last_kernel(from_first, from_second, side_geo, side_ints, ev, od, down, across, acc, known, vec,
                image, geo, ints, out, sums, side_parts, total_ref, col_x, col_y, ev_more, od_more):
    members = vec.shape[0]
    blocks = vec.shape[1] // CH - 2
    chunks = (ints[blocks] + CH - 1) // CH
    total = side_ints[0]
    per_side = side_geo.shape[1] // CH // 2

    def carry_over(i, carry):
        total_ref[:, at(i * CH)] = acc[:, at(i * CH)]
        return carry

    lax.fori_loop(0, chunks, carry_over, 0)
    for side, ref in enumerate((from_first, from_second)):

        def scale_side(h, carry, side=side, ref=ref):
            place = side * per_side + h
            scale = side_geo[2:3, at(place * CH)]
            put_split(ref[:, at(h * CH)] * scale, side_parts, place)
            return carry

        lax.fori_loop(0, side_ints[1 + side], scale_side, 0)
    held = ev.shape[0] - 1
    more = (ev_more, od_more)

    def multiply(t, which, slot):
        edge_product(t, total, down, across, side_parts, (ev, od)[which], slot, total_ref)

    sweep(total, held, None, multiply)

    def make_more(t, which, slot):
        remake(t, down, across, side_geo, geo, col_x, col_y, more[which])

    def multiply_more(t, which, slot):
        edge_product(t, total, down, across, side_parts, more[which], slot, total_ref)

    sweep_rest(total, held, make_more, multiply_more)
    zero = jnp.zeros((members, LN), F32)
    mean = known[:, 2:3]
    tail = jnp.zeros((members, 2 * LN), F32)
    for k in range(2):
        out[:, at((chunks + k) * CH)] = tail

    def sums_of(i, carry):
        zu, cross = carry
        where = at(i * CH)
        r, y = vec[:, where], image[:, where]
        yy = geo[2:3, where] * total_ref[:, where] + geo[3:4, where] * y
        out[:, where] = yy
        u = yy - mean * y
        return zu + halves((y - mean * r) * u), cross + halves(r * u)

    zu, cross = (lane_sum(x) for x in lax.fori_loop(0, chunks, sums_of, (zero, zero)))
    lane = lanes((members, LN))
    table = known[...]
    table = jnp.where(lane == 4, zu, table)
    table = jnp.where(lane == 5, cross + table, table)
    turned = jnp.concatenate([table, jnp.zeros((LN - members, LN), F32)], axis=0).T[:8]
    for k in range(sums.shape[0]):
        sums[k] = turned


def update_kernel(sums, vec, image, second, ints, count, solution_out, residual_out, solution_ref,
                  residual_ref, sems):
    members = vec.shape[0]
    blocks = vec.shape[1] // CH - 2
    chunks = (ints[blocks] + CH - 1) // CH
    terms = sums[...]
    m0 = jnp.sum(terms[:, 0, :], axis=0, keepdims=True)
    m1 = jnp.sum(terms[:, 1, :], axis=0, keepdims=True)
    used = lanes((1, LN)) < members
    m0 = jnp.where(used, m0, 1.0)
    m1 = jnp.where(used, m1, 1.0)
    mean = m1 / m0
    off = mean - terms[:, 2, :]
    vv = terms[:, 3, :] - 2.0 * off * terms[:, 6, :] + off * off * terms[:, 0, :]
    zu = terms[:, 4, :] - off * terms[:, 5, :] + off * off * terms[:, 1, :]
    cross = terms[:, 5, :] - 2.0 * off * terms[:, 1, :]
    vv, zu, cross = (jnp.sum(x, axis=0, keepdims=True) for x in (vv, zu, cross))
    alpha = m0 / m1
    rr = alpha * alpha * vv
    beta = rr / m0
    alpha_next = rr / (alpha * alpha * zu - alpha * beta * cross + beta * beta * m1)
    one = alpha + alpha_next * (1.0 + beta)
    two = alpha * alpha_next
    table = jnp.concatenate([one, two, jnp.zeros((LN - 2, LN), F32)], axis=0).T
    one, two = table[:members, 0:1], table[:members, 1:2]

    copies = []
    lane = lanes((2 * members, LN))
    for b in range(blocks):
        offset, number = ints[b], count[b]
        base = (offset // LN) * LN
        shift = offset - base
        back = lax.rem(LN - shift, LN)
        keep = lane < LN - shift
        turned = []
        for k in range(3):
            where = at(base + k * LN, LN)
            r, y, yy = vec[:, where], image[:, where], second[:, where]
            both = jnp.concatenate([one * r - two * y, r - one * y + two * yy], axis=0)
            turned.append(pltpu.roll(both, back, 1))
        for k in range(2):
            part = jnp.where(keep, turned[k], turned[k + 1])
            part = jnp.where(lane + k * LN < number, part, 0.0)
            solution_ref[b, :, k * LN : (k + 1) * LN] = part[:members]
            residual_ref[b, :, k * LN : (k + 1) * LN] = part[members:]
        for k, (src, dst) in enumerate(((solution_ref, solution_out), (residual_ref, residual_out))):
            copy = pltpu.make_async_copy(src.at[b], dst.at[b], sems.at[k, b])
            copy.start()
            copies.append(copy)
    for copy in copies:
        copy.wait()


def exchange(first, second):
    devices = lax.axis_size("region")
    received = []
    for start, block in enumerate((first, second)):
        pairs = [(i, i + 1) for i in range(start, devices - 1, 2)]
        received.append(lax.ppermute(block, "region", pairs + [(b, a) for a, b in pairs]))
    return received


def call(kernel, name, in_specs, outs, scratch=(), limit=9 * MB, cost=None):
    return pl.pallas_call(
        kernel,
        name=name,
        in_specs=in_specs,
        out_specs=[spec for spec, _ in outs],
        out_shape=[shape for _, shape in outs],
        scratch_shapes=list(scratch),
        compiler_params=pltpu.CompilerParams(vmem_limit_bytes=limit),
        cost_estimate=cost,
    )


def body(obs_pos, obs_sigma, obs_error, innovation, obs_count, pair_list, pair_live):
    blocks, members, _ = innovation.shape
    sd = jax.ShapeDtypeStruct
    in_hbm = functools.partial(pltpu.with_memory_space_constraint, memory_space=pltpu.HBM)
    in_vmem = functools.partial(pltpu.with_memory_space_constraint, memory_space=pltpu.VMEM)
    wide = blocks * CH + 2 * CH
    side_chunks = REACH + 2
    own_slots = [blocks // 2 + 1] * 2 + [OWN_HELD // 2 + 1] * 2
    side_slots = SIDE_HELD // 2 + 1
    listed = blocks * SPAN + 16
    pack_out = (VM, sd((REACH, members + 8, CH), F32))
    again_scratch = [
        pltpu.VMEM((1, CH, LN), F32),
        pltpu.VMEM((1, CH, LN), F32),
        pltpu.VMEM((1, 2 * CH, CH), BF16),
        pltpu.VMEM((1, 2 * CH, CH), BF16),
    ]
    dense = (VM, sd((members, wide), F32))
    tile = (2 * CH, CH)
    column = (VM, sd((blocks, CH, LN), F32))
    *sides, vec, geo, parts, col_x, col_y, ints, floats, down, across = call(
        prepare_kernel, "prepare", [HB] * 5,
        [
            pack_out,
            pack_out,
            dense,
            (VM, sd((8, wide), F32)),
            (VM, sd((blocks, 2 * members, CH), BF16)),
            column,
            column,
            (SM, sd((blocks + 2,), I32)),
            (SM, sd((2 * blocks + 1,), F32)),
            (SM, sd((listed,), I32)),
            (SM, sd((listed,), I32)),
        ],
        [
            pltpu.VMEM(innovation.shape, F32),
            pltpu.VMEM(obs_pos.shape, F32),
            pltpu.VMEM(obs_sigma.shape, F32),
            pltpu.VMEM(obs_error.shape, F32),
            pltpu.SMEM(obs_count.shape, I32),
            pltpu.SemaphoreType.DMA((7,)),
        ],
        limit=9 * MB,
    )(*map(in_hbm, (innovation, obs_pos, obs_sigma, obs_error, obs_count)))
    sides = exchange(*sides)
    *tiles, acc = call(
        own_kernel, "own", [VM, VM, VM, VM, SM, SM, SM],
        [(VM, pltpu.VMEM((slots,) + tile, BF16)) for slots in own_slots] + [dense],
        limit=6 * MB,
        cost=pl.CostEstimate(flops=4 * 10**9, bytes_accessed=20 * MB, transcendentals=0),
    )(geo, parts, col_x, col_y, ints, down, across)
    tiles = map(in_vmem, tiles)
    side = (VM, sd((members, REACH * CH), F32))
    (side_ev, side_od, side_geo, side_ints, side_down, side_across, image, parts,
     *image_sides) = call(
        edge_kernel, "edge", [VM, VM, VM, VM, VM, SM, SM],
        [
            (VM, pltpu.VMEM((side_slots,) + tile, BF16)),
            (VM, pltpu.VMEM((side_slots,) + tile, BF16)),
            (VM, sd((8, 2 * side_chunks * CH), F32)),
            (SM, sd((3,), I32)),
            (SM, sd((128,), I32)),
            (SM, sd((128,), I32)),
            dense,
            (VM, sd((blocks, 2 * members, CH), BF16)),
            side,
            side,
        ],
        [
            pltpu.VMEM((members, 2 * side_chunks * CH), F32),
            pltpu.VMEM((2 * side_chunks, 2 * members, CH), BF16),
            pltpu.VMEM((2 * side_chunks, CH, LN), F32),
            pltpu.VMEM((2 * side_chunks, CH, LN), F32),
            pltpu.SMEM((4 * side_chunks,), F32),
        ],
        limit=7 * MB,
    )(*sides, vec, geo, acc, ints, floats)
    side_ev, side_od = in_vmem(side_ev), in_vmem(side_od)
    image_sides = exchange(*image_sides)
    acc, known = call(
        again_kernel, "again", [VM] * 8 + [SM] * 3,
        [dense, (VM, sd((members, LN), F32))], again_scratch, limit=3 * MB,
        cost=pl.CostEstimate(flops=4 * 10**9, bytes_accessed=20 * MB, transcendentals=0),
    )(*tiles, parts, geo, vec, image, ints, down, across)
    devices = lax.axis_size("region")
    second, sums = call(
        last_kernel, "last", [VM, VM, VM, SM, VM, VM, SM, SM, VM, VM, VM, VM, VM, SM],
        [dense, (VM, sd((devices, 8, LN), F32))],
        [
            pltpu.VMEM((2 * side_chunks, 2 * members, CH), BF16),
            pltpu.VMEM((members, wide), F32),
            *again_scratch,
        ],
        limit=5 * MB,
    )(*image_sides, side_geo, side_ints, side_ev, side_od, side_down, side_across,
      acc, known, vec, image, geo, ints)
    sums = lax.all_to_all(sums, "region", 0, 0)
    field = (HB, sd((blocks, members, CH), F32))
    return tuple(call(
        update_kernel, "update", [VM, VM, VM, VM, SM, SM], [field, field],
        [
            pltpu.VMEM((blocks, members, CH), F32),
            pltpu.VMEM((blocks, members, CH), F32),
            pltpu.SemaphoreType.DMA((2, blocks)),
        ],
        limit=6 * MB,
    )(sums, vec, image, second, ints, obs_count))


def solution(mesh):
    return jax.shard_map(
        body,
        mesh=mesh,
        in_specs=(
            P(("groups", "region"), None, None),
            P(("groups", "region"), None),
            P(("groups", "region"), None),
            P(("groups", "region"), None, None),
            P(("groups", "region")),
            P(None, ("groups", "region")),
            P(("groups", "region")),
        ),
        out_specs=(P(("groups", "region"), None, None), P(("groups", "region"), None, None)),
        check_vma=False,
    )
```

profile of v0, /device:TPU:0, one launch (start us, length us, event | category | flops | bytes accessed | tf_op | source)
XLA Modules:
  0.0 54.6 jit_solution(14649412097823492829)
XLA Ops:
  0.6 3.9 %prepare.1 = (f32[5,72,256]{2,1,0:T(8,128)S(1)}, f32[5,72,256]{2,1,0:T(8,128)S(1)}, f32[64,4608]{1,0:T(8,128)S(1)}, f32[8,4608]{1,0:T(8,128)S(1)}, bf16[16,128,2...) custom-call(f32[16,64,256]{2,1,0:T(8,128)} %innov_in.1, ...), custom_call_target="tpu_custom_call" | custom-call | tf_op jit(solution)/shard_map/prepare/pallas_call | solution.py:582
  4.5 1.0 %collective-permute-start = (f32[5,72,256]{2,1,0:T(8,128)S(1)}, f32[5,72,256]{2,1,0:T(8,128)S(1)}, u32[]{:S(2)}, u32[]{:S(2)}) collective-permute-start(f32[5,72,256]{2,1,0:T(8,128)S(1)} %get-tuple-element.32), channel_id=1, source_target_pairs={{0,1},{2,3},{4,5},{6,7},{8,9},{10,11},{12,13},{14,15},{1,0},{3,2},... | collective-permute-start | bytes 1105928 | tf_op jit(solution)/shard_map/ppermute | solution.py:545
  5.6 0.7 %collective-permute-start.1 = (f32[5,72,256]{2,1,0:T(8,128)S(1)}, f32[5,72,256]{2,1,0:T(8,128)S(1)}, u32[]{:S(2)}, u32[]{:S(2)}) collective-permute-start(f32[5,72,256]{2,1,0:T(8,128)S(1)} %get-tuple-element.33), channel_id=1, source_target_pairs={{1,2},{3,4},{5,6},{7,8},{9,10},{11,12},{13,14},{2,1},{4,3},{6,5},{... | collective-permute-start | bytes 1105928 | tf_op jit(solution)/shard_map/ppermute | solution.py:545
  6.3 7.7 %own.1 = (bf16[9,512,256]{2,1,0:T(8,128)(2,1)S(1)}, bf16[9,512,256]{2,1,0:T(8,128)(2,1)S(1)}, bf16[29,512,256]{2,1,0:T(8,128)(2,1)S(1)}, bf16[29,512,256]{2,1,0:T(8,128)(2,1)S(1)}, f32[64,4608]{1,0:T(8,128)S(1)}) custom-call(f32[8,4608]{1,0:T(8,128)S(1)} %get-tuple-element.35.geo, bf16[16,128,256]{2,1,0:T(8,128)(2,1)S(1)} %get-tuple-element.36.parts, ...), custom_call_target="tpu_custom_call" | custom-call | flops 4000000000 | bytes 20971520 | tf_op jit(solution)/shard_map/own/pallas_call | solution.py:608
  14.0 0.0 collective-permute-done.from_first
  14.0 0.0 collective-permute-done.1.from_second
  14.0 3.5 %edge.1 = (bf16[13,512,256]{2,1,0:T(8,128)(2,1)S(1)}, bf16[13,512,256]{2,1,0:T(8,128)(2,1)S(1)}, f32[8,3584]{1,0:T(8,128)S(1)}, s32[3]{0:T(128)S(1)}, s32[128]{0...) custom-call(f32[5,72,256]{2,1,0:T(8,128)S(1)} %collective-permute-do, ...), custom_call_target="tpu_custom_call" | custom-call | tf_op jit(solution)/shard_map/edge/pallas_call | solution.py:617
  17.5 10.0 %collective-permute-start.2 = (f32[64,1280]{1,0:T(8,128)S(1)}, f32[64,1280]{1,0:T(8,128)S(1)}, u32[]{:S(2)}, u32[]{:S(2)}) collective-permute-start(f32[64,1280]{1,0:T(8,128)S(1)} %get-tuple-element.44), channel_id=1, source_target_pairs={{0,1},{2,3},{4,5},{6,7},{8,9},{10,11},{12,13},{14,15},{1,0},{3,2},... | collective-permute-start | bytes 983048 | tf_op jit(solution)/shard_map/ppermute | solution.py:545
  27.5 0.7 %collective-permute-start.3 = (f32[64,1280]{1,0:T(8,128)S(1)}, f32[64,1280]{1,0:T(8,128)S(1)}, u32[]{:S(2)}, u32[]{:S(2)}) collective-permute-start(f32[64,1280]{1,0:T(8,128)S(1)} %get-tuple-element.45), channel_id=1, source_target_pairs={{1,2},{3,4},{5,6},{7,8},{9,10},{11,12},{13,14},{2,1},{4,3},{6,5},{... | collective-permute-start | bytes 983048 | tf_op jit(solution)/shard_map/ppermute | solution.py:545
  28.2 4.4 %again.1 = (f32[64,4608]{1,0:T(8,128)S(1)}, f32[64,128]{1,0:T(8,128)S(1)}) custom-call(bf16[9,512,256]{2,1,0:T(8,128)(2,1)S(1)} %get-tuple-element.52.diagonal_ev, bf16[9,512,256]{2,1,0:T(8,128)(2,1)S(1)} %get-tuple-element.53.diagonal_od, bf16[29,512,256]{2,1,0:T(8,128)(2,1)S(1)} %get-tuple-element.54.ev, bf16[29,512,256]{2,1,0:T(8,128)(2,1)S(1)} %get-tuple-element.55.od, ...), custom_call_target="tpu_custom_call" | custom-call | flops 4000000000 | bytes 20971520 | tf_op jit(solution)/shard_map/again/pallas_call | solution.py:642
  32.6 0.0 collective-permute-done.2.from_first
  32.6 0.0 collective-permute-done.3.from_second
  32.6 0.0 copy-start
  32.6 1.8 %last.1 = (f32[64,4608]{1,0:T(8,128)S(1)}, f32[16,8,128]{2,1,0:T(8,128)S(1)}) custom-call(f32[64,1280]{1,0:T(8,128)S(1)} %collective-permute-done.2.from_first, f32[64,1280]{1,0:T(8,128)S(1)} %collective-permute-done.3.from_second, f32[8,3584]{1,0:T(8,128)S(1)} %get-tuple-element.46.side_geo, s32[3]{0:T(128)S(1)} %get-tuple-element.47.side_ints, ...), custom_call_target="tpu_custom_call" | custom-call | tf_op jit(solution)/shard_map/last/pallas_call | solution.py:648
  34.4 17.7 %all_to_all.5.sums = f32[16,8,128]{2,1,0:T(8,128)S(1)} all-to-all(f32[16,8,128]{2,1,0:T(8,128)S(1)} %get-tuple-element.60), channel_id=1, replica_groups=mesh['groups'=2,'region'=16] {'region'}, dimensions={0} | all-to-all | bytes 131072 | tf_op jit(solution)/shard_map/all_to_all | solution.py:659
  52.1 0.0 copy-done
  52.1 2.6 %update.1 = (f32[16,64,256]{2,1,0:T(8,128)}, f32[16,64,256]{2,1,0:T(8,128)}) custom-call(f32[16,8,128]{2,1,0:T(8,128)S(1)} %all_to_all.5.sums, f32[64,4608]{1,0:T(8,128)S(1)} %get-tuple-element.34.vec, f32[64,4608]{1,0:T(8,128)S(1)} %get-tuple-element.57.image, f32[64,4608]{1,0:T(8,128)S(1)} %get-tuple-element.61.second, s32[18]{0:T(128)S(1)} %get-tuple-element.39.ints, ...), custom_call_target="tpu_custom_call" | custom-call | tf_op jit(solution)/shard_map/update/pallas_call | solution.py:661
Async XLA Ops:
  4.5 9.5 %collective-permute-start = (f32[5,72,256]{2,1,0:T(8,128)S(1)}, f32[5,72,256]{2,1,0:T(8,128)S(1)}, u32[]{:S(2)}, u32[]{:S(2)}) collective-permute-start(f32[5,72,256]{2,1,0:T(8,128)S(1)} %get-tuple-element.32), channel_id=1, source_target_pairs={{0,1},{2,3},{4,5},{6,7},{8,9},{10,11},{12,13},{14,15},{1,0},{3,2},... | collective-permute-start | bytes 1105928 | tf_op jit(solution)/shard_map/ppermute | solution.py:545
  5.6 8.4 %collective-permute-start.1 = (f32[5,72,256]{2,1,0:T(8,128)S(1)}, f32[5,72,256]{2,1,0:T(8,128)S(1)}, u32[]{:S(2)}, u32[]{:S(2)}) collective-permute-start(f32[5,72,256]{2,1,0:T(8,128)S(1)} %get-tuple-element.33), channel_id=1, source_target_pairs={{1,2},{3,4},{5,6},{7,8},{9,10},{11,12},{13,14},{2,1},{4,3},{6,5},{... | collective-permute-start | bytes 1105928 | tf_op jit(solution)/shard_map/ppermute | solution.py:545
  17.5 15.1 %collective-permute-start.2 = (f32[64,1280]{1,0:T(8,128)S(1)}, f32[64,1280]{1,0:T(8,128)S(1)}, u32[]{:S(2)}, u32[]{:S(2)}) collective-permute-start(f32[64,1280]{1,0:T(8,128)S(1)} %get-tuple-element.44), channel_id=1, source_target_pairs={{0,1},{2,3},{4,5},{6,7},{8,9},{10,11},{12,13},{14,15},{1,0},{3,2},... | collective-permute-start | bytes 983048 | tf_op jit(solution)/shard_map/ppermute | solution.py:545
  27.5 5.1 %collective-permute-start.3 = (f32[64,1280]{1,0:T(8,128)S(1)}, f32[64,1280]{1,0:T(8,128)S(1)}, u32[]{:S(2)}, u32[]{:S(2)}) collective-permute-start(f32[64,1280]{1,0:T(8,128)S(1)} %get-tuple-element.45), channel_id=1, source_target_pairs={{1,2},{3,4},{5,6},{7,8},{9,10},{11,12},{13,14},{2,1},{4,3},{6,5},{... | collective-permute-start | bytes 983048 | tf_op jit(solution)/shard_map/ppermute | solution.py:545
  32.6 19.5 %copy-start = (s32[16]{0:T(128)S(1)}, s32[16]{0:T(128)}, u32[]{:S(2)}) copy-start(s32[16]{0:T(128)} %count.1) | copy-start | bytes 196
where the time goes:
time: 55.2 us; the launch traced here: 54.6 us
  Pallas kernels  23.9 us (43%)
  blocking collectives  17.7 us (32%)
  starting transfers between devices  12.4 us (22%)
  between operations  0.72 us (1%)
    all_to_all x1, blocking collectives, body(): sums = lax.all_to_all(sums, 'region', 0, 0)  17.7 us
    ppermute x4, starting transfers between devices, exchange(): lax.ppermute(block, 'region', pairs + [(b, a) for a, b in pairs])  12.4 us
    pallas_call x1, Pallas kernels, body(): call(own_kernel, 'own', [VM, VM, VM, VM, SM, SM, SM], [(VM, pltpu.VMEM((s...  7.73 us
    pallas_call x1, Pallas kernels, body(): call(again_kernel, 'again', [VM] * 8 + [SM] * 3, [dense, (VM, sd((members...  4.39 us
    pallas_call x1, Pallas kernels, body(): call(prepare_kernel, 'prepare', [HB] * 5, [pack_out, pack_out, dense, (VM...  3.9 us
    pallas_call x1, Pallas kernels, body(): call(edge_kernel, 'edge', [VM, VM, VM, VM, VM, SM, SM], [(VM, pltpu.VMEM(...  3.49 us
    pallas_call x1, Pallas kernels, body(): call(update_kernel, 'update', [VM, VM, VM, VM, SM, SM], [field, field], [...  2.55 us
    pallas_call x1, Pallas kernels, body(): call(last_kernel, 'last', [VM, VM, VM, SM, VM, VM, SM, SM, VM, VM, VM, VM...  1.82 us
  transfers between devices with their start and end apart: 4, of which 0 were waited for; matrix products, arithmetic and copies ran while one was open for 0% of the time, Pallas kernels for 22%

commit v1 on v0

--- a/solution.py
+++ b/solution.py
@@ -11,9 +11,9 @@
 CUTOFF_KM = 1500.0
 SCALE_KM = 1000.0
 LOG2E = 1.4426950408889634
-UNIT = LOG2E / SCALE_KM
-TAPER = 1.0 / (CUTOFF_KM * UNIT)
-LIMIT = CUTOFF_KM * UNIT
+UNIT = 1.0 / CUTOFF_KM
+DECAY = -LOG2E * CUTOFF_KM / SCALE_KM
+LIMIT = 1.0
 CH = 256
 LN = 128
 GROUP = 4
@@ -75,8 +75,8 @@
             dy = col_y[place, top : top + strip, :] - row_y[:, left : left + LN]
             square = jnp.maximum(dx * dx + dy * dy, TINY)
             distance = square * lax.rsqrt(square)
-            tapered = jnp.maximum(1.0 - distance * TAPER, 0.0)
-            value = jnp.exp2(-distance) * (tapered * tapered)
+            tapered = jnp.maximum(1.0 - distance, 0.0)
+            value = jnp.exp2(distance * DECAY) * (tapered * tapered)
             high, low = split(value)
             tile_ref[slot, top : top + strip, left : left + LN] = high
             tile_ref[slot, CH + top : CH + top + strip, left : left + LN] = low
@@ -91,24 +91,26 @@
     return wide[:half] + wide[half:] + fine
 
 
-def own_product(t, total, down, across, parts_ref, tile_ref, slot, acc):
+def counted(value, t, total, sure):
+    return value if sure else (t < total).astype(F32) * value
+
+
+def own_product(t, total, down, across, parts_ref, tile_ref, slot, acc, sure=False):
     i, j = down[t], across[t]
-    here = (t < total).astype(F32)
     forward = product(parts_ref, i, tile_ref, slot, False)
     backward = product(parts_ref, j, tile_ref, slot, True)
-    acc[:, at(j * CH)] += here * forward
-    acc[:, at(i * CH)] += here * backward
-
-
-def diagonal_product(t, total, parts_ref, tile_ref, slot, acc):
-    here = (t < total).astype(F32)
+    acc[:, at(j * CH)] += counted(forward, t, total, sure)
+    acc[:, at(i * CH)] += counted(backward, t, total, sure)
+
+
+def diagonal_product(t, total, parts_ref, tile_ref, slot, acc, sure=False):
     i = jnp.minimum(t, total - 1)
-    acc[:, at(i * CH)] += here * product(parts_ref, i, tile_ref, slot, False)
-
-
-def edge_product(t, total, down, across, parts_ref, tile_ref, slot, acc):
-    here = (t < total).astype(F32)
-    acc[:, at(across[t] * CH)] += here * product(parts_ref, down[t], tile_ref, slot, False)
+    acc[:, at(i * CH)] += counted(product(parts_ref, i, tile_ref, slot, False), t, total, sure)
+
+
+def edge_product(t, total, down, across, parts_ref, tile_ref, slot, acc, sure=False):
+    value = product(parts_ref, down[t], tile_ref, slot, False)
+    acc[:, at(across[t] * CH)] += counted(value, t, total, sure)
 
 
 def sweep(total, held, make, multiply):
@@ -116,7 +118,7 @@
     full = jnp.minimum(total, 2 * held) // BATCH
 
     def many(p, carry):
-        for half in (make, multiply):
+        for half in (make, functools.partial(multiply, sure=True)):
             for u in range(BATCH):
                 if half is not None:
                     half(BATCH * p + u, u % 2, BATCH // 2 * p + u // 2)
@@ -156,8 +158,8 @@
                    parts, col_x, col_y, ints, floats, down, across, innov, pos, sigma, err, count,
                    sems):
     blocks, members = innov.shape[0], innov.shape[1]
-    odd = lax.rem(lax.axis_index("region"), 2)
-    starts = ((1 - odd) * (blocks - REACH), odd * (blocks - REACH))
+    even = 1 - lax.rem(lax.axis_index("region"), 2)
+    starts = ((1 - even) * (blocks - REACH), even * (blocks - REACH))
     ends = tuple(zip(starts, (first_out, second_out)))
     small = [(pos_in, pos), (sigma_in, sigma), (err_in, err), (count_in, count)]
     large = [(innov_in, innov)]
@@ -253,16 +255,16 @@
         i = jnp.minimum(t, chunks - 1)
         build_at(i, i, (diagonal_ev, diagonal_od)[which], slot)
 
-    def multiply_diagonal(t, which, slot):
-        diagonal_product(t, chunks, parts, (diagonal_ev, diagonal_od)[which], slot, acc)
+    def multiply_diagonal(t, which, slot, sure=False):
+        diagonal_product(t, chunks, parts, (diagonal_ev, diagonal_od)[which], slot, acc, sure)
 
     sweep(chunks, blocks // 2, make_diagonal, multiply_diagonal)
 
     def make(t, which, slot):
         build_at(down[t], across[t], (ev, od)[which], slot)
 
-    def multiply(t, which, slot):
-        own_product(t, total, down, across, parts, (ev, od)[which], slot, acc)
+    def multiply(t, which, slot, sure=False):
+        own_product(t, total, down, across, parts, (ev, od)[which], slot, acc, sure)
 
     sweep(total, ev.shape[0] - 1, make, multiply)
 
@@ -278,7 +280,7 @@
     origin = floats[0]
     out[...] = jnp.zeros_like(out)
     side_ends = []
-    odd = lax.rem(lax.axis_index("region"), 2)
+    even = 1 - lax.rem(lax.axis_index("region"), 2)
     for side, ref in enumerate((from_first, from_second)):
         offset = jnp.int32(side * wide)
         for b in range(REACH):
@@ -311,7 +313,7 @@
     lax.fori_loop(0, (jnp.maximum(*side_chunks) + 1) // 2, prepare, 0)
     total = jnp.int32(0)
     for side in range(2):
-        ahead = odd == side
+        ahead = even == side
 
         def enlist(h, t, side=side, ahead=ahead):
             place = side * (wide // CH) + h
@@ -336,8 +338,8 @@
         where = at(across[t] * CH)
         build(col_x, col_y, down[t], geo[0:1, where], geo[1:2, where], (ev, od)[which], slot)
 
-    def multiply(t, which, slot):
-        edge_product(t, total, down, across, side_parts, (ev, od)[which], slot, out)
+    def multiply(t, which, slot, sure=False):
+        edge_product(t, total, down, across, side_parts, (ev, od)[which], slot, out, sure)
 
     sweep(total, ev.shape[0] - 1, make, multiply)
 
@@ -351,7 +353,7 @@
 
     lax.fori_loop(0, chunks, finish, 0)
     tail = ints[blocks - REACH]
-    for start, dst in (((1 - odd) * tail, first_out), (odd * tail, second_out)):
+    for start, dst in (((1 - even) * tail, first_out), (even * tail, second_out)):
         base = (start // LN) * LN
         shift = start - base
         back = lax.rem(LN - shift, LN)
@@ -380,13 +382,13 @@
     more = (ev_more, od_more)
     chunks = (ints[blocks] + CH - 1) // CH
 
-    def multiply_diagonal(t, which, slot):
-        diagonal_product(t, chunks, parts, (diagonal_ev, diagonal_od)[which], slot, acc)
+    def multiply_diagonal(t, which, slot, sure=False):
+        diagonal_product(t, chunks, parts, (diagonal_ev, diagonal_od)[which], slot, acc, sure)
 
     sweep(chunks, blocks // 2, None, multiply_diagonal)
 
-    def multiply(t, which, slot):
-        own_product(t, total, down, across, parts, (ev, od)[which], slot, acc)
+    def multiply(t, which, slot, sure=False):
+        own_product(t, total, down, across, parts, (ev, od)[which], slot, acc, sure)
 
     sweep(total, held, None, multiply)
 
@@ -447,8 +449,8 @@
     held = ev.shape[0] - 1
     more = (ev_more, od_more)
 
-    def multiply(t, which, slot):
-        edge_product(t, total, down, across, side_parts, (ev, od)[which], slot, total_ref)
+    def multiply(t, which, slot, sure=False):
+        edge_product(t, total, down, across, side_parts, (ev, od)[which], slot, total_ref, sure)
 
     sweep(total, held, None, multiply)
 
@@ -540,7 +542,7 @@
 def exchange(first, second):
     devices = lax.axis_size("region")
     received = []
-    for start, block in enumerate((first, second)):
+    for start, block in ((1, first), (0, second)):
         pairs = [(i, i + 1) for i in range(start, devices - 1, 2)]
         received.append(lax.ppermute(block, "region", pairs + [(b, a) for a, b in pairs]))
     return received

time: 55.2 us -> 53.4 us (0.967)
  blocking collectives: 17.7 us -> 15.4 us
  starting transfers between devices: 12.4 us -> 13.5 us
    all_to_all x1, blocking collectives: 17.7 us -> 15.4 us  [body(): sums = lax.all_to_all(sums, 'region', 0, 0)]
    ppermute x4, starting transfers between devices: 12.4 us -> 13.5 us  [exchange(): lax.ppermute(block, 'region', pairs + [(b, a) for a, b in pairs])]
    pallas_call x1, Pallas kernels: 7.73 us -> 6.84 us  [body(): call(own_kernel, 'own', [VM, VM, VM, VM, SM, SM, SM], [(VM, pltpu.VMEM((s...]
  transfers between devices with their start and end apart: 4 -> 4, of which waited for: 0 -> 0; matrix products, arithmetic and copies ran while one was open for 0% -> 0% of each run, Pallas kernels for 22% -> 20%
where the time goes in v1:
time: 53.4 us; the launch traced here: 53 us
  Pallas kernels  23.4 us (44%)
  blocking collectives  15.4 us (29%)
  starting transfers between devices  13.5 us (25%)
  between operations  0.72 us (1%)
    all_to_all x1, blocking collectives, body(): sums = lax.all_to_all(sums, 'region', 0, 0)  15.4 us
    ppermute x4, starting transfers between devices, exchange(): lax.ppermute(block, 'region', pairs + [(b, a) for a, b in pairs])  13.5 us
    pallas_call x1, Pallas kernels, body(): call(own_kernel, 'own', [VM, VM, VM, VM, SM, SM, SM], [(VM, pltpu.VMEM((s...  6.84 us
    pallas_call x1, Pallas kernels, body(): call(edge_kernel, 'edge', [VM, VM, VM, VM, VM, SM, SM], [(VM, pltpu.VMEM(...  4.04 us
    pallas_call x1, Pallas kernels, body(): call(again_kernel, 'again', [VM] * 8 + [SM] * 3, [dense, (VM, sd((members...  4.01 us
    pallas_call x1, Pallas kernels, body(): call(prepare_kernel, 'prepare', [HB] * 5, [pack_out, pack_out, dense, (VM...  3.9 us
    pallas_call x1, Pallas kernels, body(): call(update_kernel, 'update', [VM, VM, VM, VM, SM, SM], [field, field], [...  2.55 us
    pallas_call x1, Pallas kernels, body(): call(last_kernel, 'last', [VM, VM, VM, SM, VM, VM, SM, SM, VM, VM, VM, VM...  2.05 us
  transfers between devices with their start and end apart: 4, of which 0 were waited for; matrix products, arithmetic and copies ran while one was open for 0% of the time, Pallas kernels for 20%

profile of v1, /device:TPU:0, one launch (start us, length us, event | category | flops | bytes accessed | tf_op | source)
XLA Modules:
  0.0 53.0 jit_solution(11446871720833512505)
XLA Ops:
  0.6 3.9 %prepare.1 = (f32[5,72,256]{2,1,0:T(8,128)S(1)}, f32[5,72,256]{2,1,0:T(8,128)S(1)}, f32[64,4608]{1,0:T(8,128)S(1)}, f32[8,4608]{1,0:T(8,128)S(1)}, bf16[16,128,2...) custom-call(f32[16,64,256]{2,1,0:T(8,128)} %innov_in.1, ...), custom_call_target="tpu_custom_call" | custom-call | tf_op jit(solution)/shard_map/prepare/pallas_call | solution.py:584
  4.5 0.7 %collective-permute-start = (f32[5,72,256]{2,1,0:T(8,128)S(1)}, f32[5,72,256]{2,1,0:T(8,128)S(1)}, u32[]{:S(2)}, u32[]{:S(2)}) collective-permute-start(f32[5,72,256]{2,1,0:T(8,128)S(1)} %get-tuple-element.32), channel_id=1, source_target_pairs={{1,2},{3,4},{5,6},{7,8},{9,10},{11,12},{13,14},{2,1},{4,3},{6,5},{... | collective-permute-start | bytes 1105928 | tf_op jit(solution)/shard_map/ppermute | solution.py:547
  5.2 4.4 %collective-permute-start.1 = (f32[5,72,256]{2,1,0:T(8,128)S(1)}, f32[5,72,256]{2,1,0:T(8,128)S(1)}, u32[]{:S(2)}, u32[]{:S(2)}) collective-permute-start(f32[5,72,256]{2,1,0:T(8,128)S(1)} %get-tuple-element.33), channel_id=1, source_target_pairs={{0,1},{2,3},{4,5},{6,7},{8,9},{10,11},{12,13},{14,15},{1,0},{3,2},... | collective-permute-start | bytes 1105928 | tf_op jit(solution)/shard_map/ppermute | solution.py:547
  9.6 6.8 %own.1 = (bf16[9,512,256]{2,1,0:T(8,128)(2,1)S(1)}, bf16[9,512,256]{2,1,0:T(8,128)(2,1)S(1)}, bf16[29,512,256]{2,1,0:T(8,128)(2,1)S(1)}, bf16[29,512,256]{2,1,0:T(8,128)(2,1)S(1)}, f32[64,4608]{1,0:T(8,128)S(1)}) custom-call(f32[8,4608]{1,0:T(8,128)S(1)} %get-tuple-element.35.geo, bf16[16,128,256]{2,1,0:T(8,128)(2,1)S(1)} %get-tuple-element.36.parts, ...), custom_call_target="tpu_custom_call" | custom-call | flops 4000000000 | bytes 20971520 | tf_op jit(solution)/shard_map/own/pallas_call | solution.py:610
  16.4 0.0 collective-permute-done.from_first
  16.5 0.0 collective-permute-done.1.from_second
  16.5 4.0 %edge.1 = (bf16[13,512,256]{2,1,0:T(8,128)(2,1)S(1)}, bf16[13,512,256]{2,1,0:T(8,128)(2,1)S(1)}, f32[8,3584]{1,0:T(8,128)S(1)}, s32[3]{0:T(128)S(1)}, s32[128]{0...) custom-call(f32[5,72,256]{2,1,0:T(8,128)S(1)} %collective-permute-do, ...), custom_call_target="tpu_custom_call" | custom-call | tf_op jit(solution)/shard_map/edge/pallas_call | solution.py:619
  20.5 0.7 %collective-permute-start.2 = (f32[64,1280]{1,0:T(8,128)S(1)}, f32[64,1280]{1,0:T(8,128)S(1)}, u32[]{:S(2)}, u32[]{:S(2)}) collective-permute-start(f32[64,1280]{1,0:T(8,128)S(1)} %get-tuple-element.44), channel_id=1, source_target_pairs={{1,2},{3,4},{5,6},{7,8},{9,10},{11,12},{13,14},{2,1},{4,3},{6,5},{... | collective-permute-start | bytes 983048 | tf_op jit(solution)/shard_map/ppermute | solution.py:547
  21.2 7.8 %collective-permute-start.3 = (f32[64,1280]{1,0:T(8,128)S(1)}, f32[64,1280]{1,0:T(8,128)S(1)}, u32[]{:S(2)}, u32[]{:S(2)}) collective-permute-start(f32[64,1280]{1,0:T(8,128)S(1)} %get-tuple-element.45), channel_id=1, source_target_pairs={{0,1},{2,3},{4,5},{6,7},{8,9},{10,11},{12,13},{14,15},{1,0},{3,2},... | collective-permute-start | bytes 983048 | tf_op jit(solution)/shard_map/ppermute | solution.py:547
  29.0 4.0 %again.1 = (f32[64,4608]{1,0:T(8,128)S(1)}, f32[64,128]{1,0:T(8,128)S(1)}) custom-call(bf16[9,512,256]{2,1,0:T(8,128)(2,1)S(1)} %get-tuple-element.52.diagonal_ev, bf16[9,512,256]{2,1,0:T(8,128)(2,1)S(1)} %get-tuple-element.53.diagonal_od, bf16[29,512,256]{2,1,0:T(8,128)(2,1)S(1)} %get-tuple-element.54.ev, bf16[29,512,256]{2,1,0:T(8,128)(2,1)S(1)} %get-tuple-element.55.od, ...), custom_call_target="tpu_custom_call" | custom-call | flops 4000000000 | bytes 20971520 | tf_op jit(solution)/shard_map/again/pallas_call | solution.py:644
  33.0 0.0 collective-permute-done.2.from_first
  33.0 0.0 collective-permute-done.3.from_second
  33.0 0.0 copy-start
  33.0 2.1 %last.1 = (f32[64,4608]{1,0:T(8,128)S(1)}, f32[16,8,128]{2,1,0:T(8,128)S(1)}) custom-call(f32[64,1280]{1,0:T(8,128)S(1)} %collective-permute-done.2.from_first, f32[64,1280]{1,0:T(8,128)S(1)} %collective-permute-done.3.from_second, f32[8,3584]{1,0:T(8,128)S(1)} %get-tuple-element.46.side_geo, s32[3]{0:T(128)S(1)} %get-tuple-element.47.side_ints, ...), custom_call_target="tpu_custom_call" | custom-call | tf_op jit(solution)/shard_map/last/pallas_call | solution.py:650
  35.1 15.4 %all_to_all.5.sums = f32[16,8,128]{2,1,0:T(8,128)S(1)} all-to-all(f32[16,8,128]{2,1,0:T(8,128)S(1)} %get-tuple-element.60), channel_id=1, replica_groups=mesh['groups'=2,'region'=16] {'region'}, dimensions={0} | all-to-all | bytes 131072 | tf_op jit(solution)/shard_map/all_to_all | solution.py:661
  50.5 0.0 copy-done
  50.5 2.5 %update.1 = (f32[16,64,256]{2,1,0:T(8,128)}, f32[16,64,256]{2,1,0:T(8,128)}) custom-call(f32[16,8,128]{2,1,0:T(8,128)S(1)} %all_to_all.5.sums, f32[64,4608]{1,0:T(8,128)S(1)} %get-tuple-element.34.vec, f32[64,4608]{1,0:T(8,128)S(1)} %get-tuple-element.57.image, f32[64,4608]{1,0:T(8,128)S(1)} %get-tuple-element.61.second, s32[18]{0:T(128)S(1)} %get-tuple-element.39.ints, ...), custom_call_target="tpu_custom_call" | custom-call | tf_op jit(solution)/shard_map/update/pallas_call | solution.py:663
Async XLA Ops:
  4.5 11.9 %collective-permute-start = (f32[5,72,256]{2,1,0:T(8,128)S(1)}, f32[5,72,256]{2,1,0:T(8,128)S(1)}, u32[]{:S(2)}, u32[]{:S(2)}) collective-permute-start(f32[5,72,256]{2,1,0:T(8,128)S(1)} %get-tuple-element.32), channel_id=1, source_target_pairs={{1,2},{3,4},{5,6},{7,8},{9,10},{11,12},{13,14},{2,1},{4,3},{6,5},{... | collective-permute-start | bytes 1105928 | tf_op jit(solution)/shard_map/ppermute | solution.py:547
  5.2 11.2 %collective-permute-start.1 = (f32[5,72,256]{2,1,0:T(8,128)S(1)}, f32[5,72,256]{2,1,0:T(8,128)S(1)}, u32[]{:S(2)}, u32[]{:S(2)}) collective-permute-start(f32[5,72,256]{2,1,0:T(8,128)S(1)} %get-tuple-element.33), channel_id=1, source_target_pairs={{0,1},{2,3},{4,5},{6,7},{8,9},{10,11},{12,13},{14,15},{1,0},{3,2},... | collective-permute-start | bytes 1105928 | tf_op jit(solution)/shard_map/ppermute | solution.py:547
  20.5 12.5 %collective-permute-start.2 = (f32[64,1280]{1,0:T(8,128)S(1)}, f32[64,1280]{1,0:T(8,128)S(1)}, u32[]{:S(2)}, u32[]{:S(2)}) collective-permute-start(f32[64,1280]{1,0:T(8,128)S(1)} %get-tuple-element.44), channel_id=1, source_target_pairs={{1,2},{3,4},{5,6},{7,8},{9,10},{11,12},{13,14},{2,1},{4,3},{6,5},{... | collective-permute-start | bytes 983048 | tf_op jit(solution)/shard_map/ppermute | solution.py:547
  21.2 11.8 %collective-permute-start.3 = (f32[64,1280]{1,0:T(8,128)S(1)}, f32[64,1280]{1,0:T(8,128)S(1)}, u32[]{:S(2)}, u32[]{:S(2)}) collective-permute-start(f32[64,1280]{1,0:T(8,128)S(1)} %get-tuple-element.45), channel_id=1, source_target_pairs={{0,1},{2,3},{4,5},{6,7},{8,9},{10,11},{12,13},{14,15},{1,0},{3,2},... | collective-permute-start | bytes 983048 | tf_op jit(solution)/shard_map/ppermute | solution.py:547
  33.0 17.5 %copy-start = (s32[16]{0:T(128)S(1)}, s32[16]{0:T(128)}, u32[]{:S(2)}) copy-start(s32[16]{0:T(128)} %count.1) | copy-start | bytes 196
